TPU v7x, 32 devices: a whole 2x2x4 slice. The times are simulated.
32 devices in a mesh: groups: 2 (over y), segment: 2 (over core), seq: 8 (over z, x).
Axes of the slice: x: 2, y: 2, z: 4, core: 2. Of those that a mesh axis runs over, the one named last changes fastest.
Arguments:
- held: bfloat16 [2, 32, 8, 16, 640], P('segment', ('groups', 'seq')), parts along dimension 1, may hold values from -6 to 6
- arrivals: bfloat16 [3, 32, 8, 16, 640], P(None, ('groups', 'seq')), parts along dimension 1, may hold values from -6 to 6
- spatial_weight: bfloat16 [2, 9, 640, 640], P('segment'), may hold values from -0.078125 to 0.078125
- spatial_scale: float32 [2, 5, 640], P('segment'), may hold values from 0.5 to 2
- temporal_weight: bfloat16 [2, 3, 640, 640], P('segment'), may hold values from -0.125 to 0.125
- temporal_scale: float32 [2, 5, 640], P('segment'), may hold values from 0.5 to 2
Outputs:
- emitted: bfloat16 [2, 4, 32, 8, 16, 640], P('segment', None, ('groups', 'seq')), parts along dimension 2
There are 2 independent parts, one for each index of `groups`. A program takes and returns all parts, laid end to end along the dimension named above; an argument that names none is the same for every part. Nothing has to cross between parts.
All inputs are finite; a program needn't handle non-finite values.
Results may differ from a plain program's by a relative error of at most 0.014.
Values may be sent and summed in bfloat16 or wider, within the bound.
A program may use at most 128 MiB of HBM per device.

v0:
```python
import jax
import jax.numpy as jnp
from jax import lax
from jax.sharding import PartitionSpec as P


def with_halo(cells, sides, width):
    for axis, dim in sides:
        count = lax.axis_size(axis)
        ends = count - 1
        head = lax.slice_in_dim(cells, 0, width, axis=dim)
        tail = lax.slice_in_dim(cells, cells.shape[dim] - width, cells.shape[dim], axis=dim)
        cells = jnp.concatenate(
            [
                lax.ppermute(tail, axis, [(i, (i + 1) % count) for i in range(ends)]),
                cells,
                lax.ppermute(head, axis, [((i + 1) % count, i) for i in range(ends)]),
            ],
            axis=dim,
        )
    return cells


def passed_along(value, axis, steps):
    count = lax.axis_size(axis)
    initial, last = (max(0, -steps), min(count, count - steps))
    return lax.ppermute(value, axis, [(source, source + steps) for source in range(initial, last)])


def dequantize(weights, scales):
    block = weights.shape[1] // scales.shape[0]
    expanded = jnp.repeat(scales, block, axis=0)
    return (weights.astype(jnp.float32) * expanded[None]).astype(jnp.bfloat16)


def spatial_term(activation, kernels):
    frames, height, width, channels = activation.shape
    padded = jnp.pad(activation, ((0, 0), (1, 1), (1, 1), (0, 0)))
    total = jnp.zeros((frames * height * width, channels), jnp.float32)
    for row_tap in range(3):
        for col_tap in range(3):
            window = padded[:, row_tap : row_tap + height, col_tap : col_tap + width].reshape(
                -1, channels
            )
            total = total + jnp.dot(
                window, kernels[row_tap * 3 + col_tap], preferred_element_type=jnp.float32
            )
    return total.reshape(activation.shape)


def section_local(activation, spatial_kernels, temporal_kernels):
    lifted = jax.nn.silu(activation.astype(jnp.float32)).astype(jnp.bfloat16)
    middle = (activation.astype(jnp.float32) + spatial_term(lifted, spatial_kernels)).astype(
        jnp.bfloat16
    )
    lifted_mid = jax.nn.silu(middle.astype(jnp.float32)).astype(jnp.bfloat16)
    frames_dev, height, width, channels = lifted_mid.shape
    extended = with_halo(lifted_mid, (("seq", 0),), 1)
    total = jnp.zeros((frames_dev * height * width, channels), jnp.float32)
    for frame_tap in range(3):
        window = extended[frame_tap : frame_tap + frames_dev].reshape(-1, channels)
        total = total + jnp.dot(
            window, temporal_kernels[frame_tap], preferred_element_type=jnp.float32
        )
    temporal = total.reshape(lifted_mid.shape).astype(jnp.bfloat16)
    return (middle.astype(jnp.float32) + temporal.astype(jnp.float32)).astype(jnp.bfloat16)


def local(held, arrivals, spatial_weight, spatial_scale, temporal_weight, temporal_scale):
    spatial_kernels = dequantize(spatial_weight[0], spatial_scale[0])
    temporal_kernels = dequantize(temporal_weight[0], temporal_scale[0])
    first_segment = lax.axis_index("segment") == 0
    ticks = arrivals.shape[0] + 1
    current = held[0]
    collected = []
    for tick_index in range(ticks):
        current = section_local(current, spatial_kernels, temporal_kernels)
        collected.append(current)
        if tick_index + 1 < ticks:
            moved = passed_along(current, "segment", 1)
            current = jnp.where(first_segment, arrivals[tick_index], moved)
    return jnp.stack(collected)[None]


def solution(mesh):
    in_specs = (
        P("segment", ("groups", "seq"), None, None, None),
        P(None, ("groups", "seq"), None, None, None),
        P("segment", None, None, None),
        P("segment", None, None),
        P("segment", None, None, None),
        P("segment", None, None),
    )
    out_specs = P("segment", None, ("groups", "seq"), None, None, None)
    return jax.shard_map(local, mesh=mesh, in_specs=in_specs, out_specs=out_specs, check_vma=False)
```

profile of v0, /device:TPU:17, one launch (start us, length us, event | category | flops | bytes accessed | tf_op | source)
XLA Modules:
  0.0 105.6 jit_solution(9680626531610827760)
XLA Ops:
  0.0 1.2 %fusion.59 = bf16[2,8,16,640]{3,2,1,0:T(8,128)(2,1)S(1)} fusion(bf16[1,2,8,16,640]{4,3,2,1,0:T(8,128)(2,1)} %param.6), kind=kLoop, calls=%fused_computation.172 | loop fusion | flops 983040 | bytes 655360 | tf_op jit(solution)/shard_map/convert_element_type | solution.py:52
  1.2 1.2 %fusion.54 = bf16[1,2,8,16,640]{4,3,2,1,0:T(8,128)(2,1)S(1)} fusion(bf16[1,2,8,16,640]{4,3,2,1,0:T(8,128)(2,1)} %param.6), kind=kLoop, calls=%fused_computation.167 | loop fusion | flops 983040 | bytes 655360 | tf_op jit(solution)/shard_map/convert_element_type | solution.py:52
  2.3 0.7 copy.12
  3.1 1.5 %pad_slice_fusion.24 = (bf16[2,8,16,640]{3,2,1,0:T(8,128)(2,1)}, bf16[2,8,16,640]{3,2,1,0:T(8,128)(2,1)S(1)}, bf16[2,8,16,640]{3,2,1,0:T(8,128)(2,1)}, bf16[2,8,...) fusion(bf16[2,8,16,640]{3,2,1,0:T(8,128)(2,1)S(1)} %fusion.59), kind=kLoop, calls=%fused_computation.74 | loop fusion | bytes 2949120 | tf_op jit(solution)/shard_map/slice | solution.py:42
  4.5 1.3 %broadcast_in_dim.9 = f32[5,128,640]{2,1,0:T(8,128)} broadcast(f32[5,640]{1,0:T(8,128)S(1)} %bitcast.310), dimensions={0,2} | broadcast | bytes 1651200 | tf_op jit(solution)/shard_map/broadcast_in_dim | solution.py:32
  5.8 5.0 %fusion = bf16[9,640,640]{2,1,0:T(8,128)(2,1)S(1)} fusion(bf16[1,9,640,640]{3,2,1,0:T(8,128)(2,1)} %param.8, f32[640,640]{1,0:T(8,128)} %bitcast.252), kind=kLoop, calls=%fused_computation.1 | loop fusion | flops 11059200 | bytes 16384000 | tf_op jit(solution)/shard_map/convert_element_type | solution.py:33
  10.8 1.8 %fusion.64 = f32[256,640]{1,0:T(8,128)S(1)} fusion(bf16[256,640]{1,0:T(8,128)(2,1)} %bitcast.291, bf16[9,640,640]{2,1,0:T(8,128)(2,1)S(1)} %fusion), kind=kOutput, calls=%fused_computation.178 | convolution fusion | flops 209715200 | bytes 1802240 | tf_op jit(solution)/shard_map/dot_general | solution.py:45
  13.1 1.8 %convolution_add_fusion.34 = f32[256,640]{1,0:T(8,128)S(1)} fusion(f32[256,640]{1,0:T(8,128)S(1)} %convolution_add_fusion.35, bf16[256,640]{1,0:T(8,128)(2,1)} %bitcast.289, bf16[9,640,640]{2,1,0:T(8,128)(2,1)S(1)} %fusion), kind=kOutput, calls=%fused_computation.39 | convolution fusion | flops 209879040 | bytes 2457600 | tf_op jit(solution)/shard_map/dot_general | solution.py:45
  14.9 1.4 %convolution_add_fusion.33 = f32[256,640]{1,0:T(8,128)S(1)} fusion(f32[256,640]{1,0:T(8,128)S(1)} %convolution_add_fusion.34, bf16[256,640]{1,0:T(8,128)(2,1)} %bitcast.285, bf16[9,640,640]{2,1,0:T(8,128)(2,1)S(1)} %fusion), kind=kOutput, calls=%fused_computation.38 | convolution fusion | flops 209879040 | bytes 2457600 | tf_op jit(solution)/shard_map/dot_general | solution.py:45
  16.8 0.5 convolution_add_fusion.31
  17.3 0.5 convolution_add_fusion.30
  17.8 0.5 convolution_add_fusion.29
  18.3 0.5 fusion.50
  19.0 3.1 %collective-permute-start = (bf16[1,8,16,640]{3,2,1,0:T(8,128)(2,1)S(1)}, bf16[1,8,16,640]{3,2,1,0:T(8,128)(2,1)S(1)}, u32[]{:S(2)}, u32[]{:S(2)}) collective-permute-start(bf16[1,8,16,640]{3,2,1,0:T(8,128)(2,1)S(1)} %get-tuple-element.49), channel_id=1, source_target_pairs={{0,1},{1,2},{2,3},{3,4},{4,5},{5,6},{6,7},{8,9},{9,10},{10,11},{11... | collective-permute-start | bytes 491528 | tf_op jit(solution)/shard_map/ppermute | solution.py:15
  22.2 3.1 %collective-permute-start.1 = (bf16[1,8,16,640]{3,2,1,0:T(8,128)(2,1)S(1)}, bf16[1,8,16,640]{3,2,1,0:T(8,128)(2,1)S(1)}, u32[]{:S(2)}, u32[]{:S(2)}) collective-permute-start(bf16[1,8,16,640]{3,2,1,0:T(8,128)(2,1)S(1)} %get-tuple-element.50), channel_id=1, source_target_pairs={{1,0},{2,1},{3,2},{4,3},{5,4},{6,5},{7,6},{9,8},{10,9},{11,10},{12... | collective-permute-start | bytes 491528 | tf_op jit(solution)/shard_map/ppermute | solution.py:17
  25.4 0.5 fusion.1
  25.9 0.5 fusion.68
  26.4 0.5 collective-permute-done
  26.9 4.5 %collective-permute-done.1 = bf16[1,8,16,640]{3,2,1,0:T(8,128)(2,1)S(1)} collective-permute-done((bf16[1,8,16,640]{3,2,1,0:T(8,128)(2,1)S(1)}, bf16[1,8,16,640]{3,2,1,0:T(8,128)(2,1)S(1)}, u32[]{:S(2)}, u32[]{:S(2)}) %collective-permute-start.1) | collective-permute-done | bytes 163872 | tf_op jit(solution)/shard_map/ppermute | solution.py:17
  32.0 0.5 fusion.10
  32.5 0.9 fusion.19
  33.4 1.3 %collective-permute-start.2 = (bf16[2,8,16,640]{3,2,1,0:T(8,128)(2,1)}, bf16[2,8,16,640]{3,2,1,0:T(8,128)(2,1)}, u32[]{:S(2)}, u32[]{:S(2)}) collective-permute-start(bf16[2,8,16,640]{3,2,1,0:T(8,128)(2,1)} %fusion.19), channel_id=1, source_target_pairs={{0,8},{1,9},{2,10},{3,11},{4,12},{5,13},{6,14},{7,15},{16,24},{17,... | collective-permute-start | bytes 983048 | tf_op jit(solution)/shard_map/ppermute | solution.py:27
  34.7 2.5 %collective-permute-done.2 = bf16[2,8,16,640]{3,2,1,0:T(8,128)(2,1)} collective-permute-done((bf16[2,8,16,640]{3,2,1,0:T(8,128)(2,1)}, bf16[2,8,16,640]{3,2,1,0:T(8,128)(2,1)}, u32[]{:S(2)}, u32[]{:S(2)}) %collective-permute-start.2) | collective-permute-done | bytes 327712 | tf_op jit(solution)/shard_map/ppermute | solution.py:27
  37.3 1.3 %fusion.23 = bf16[2,8,16,640]{3,2,1,0:T(8,128)(2,1)S(1)} fusion(bf16[2,8,16,640]{3,2,1,0:T(8,128)(2,1)} %collective-permute-done.2, bf16[3,2,8,16,640]{4,3,2,1,0:T(8,128)(2,1)} %param.7, pred[]{:T(512)S(6)} %eq.3), kind=kLoop, calls=%fused_computation.129 | loop fusion | flops 1146880 | bytes 983041 | tf_op jit(solution)/shard_map/convert_element_type | solution.py:52
  38.8 1.6 %fusion.63 = f32[256,640]{1,0:T(8,128)S(1)} fusion(bf16[256,640]{1,0:T(8,128)(2,1)S(1)} %bitcast.301, bf16[9,640,640]{2,1,0:T(8,128)(2,1)} %copy-done), kind=kOutput, calls=%fused_computation.177 | convolution fusion | flops 209715200 | bytes 1802240 | tf_op jit(solution)/shard_map/dot_general | solution.py:45
  40.4 1.6 %convolution_add_fusion.26 = f32[256,640]{1,0:T(8,128)S(1)} fusion(f32[256,640]{1,0:T(8,128)S(1)} %fusion.63, bf16[256,640]{1,0:T(8,128)(2,1)S(1)} %bitcast.298, bf16[9,640,640]{2,1,0:T(8,128)(2,1)} %copy-done), kind=kOutput, calls=%fused_computation.31 | convolution fusion | flops 209879040 | bytes 2457600 | tf_op jit(solution)/shard_map/dot_general | solution.py:45
  43.0 0.5 convolution_add_fusion.23
  45.4 1.2 %fusion.28 = (bf16[2,8,16,640]{3,2,1,0:T(8,128)(2,1)S(1)}, bf16[2,8,16,640]{3,2,1,0:T(8,128)(2,1)S(1)}) fusion(f32[2,8,16,640]{3,2,1,0:T(8,128)S(1)} %bitcast.262, bf16[2,8,16,640]{3,2,1,0:T(8,128)(2,1)} %collective-permute-done.2, bf16[3,2,8,16,640]{4,3,2,1,0:T(8,128)(2,1)S(1)} %copy-done.8, pred[]{:T(512)S(6)} %eq.3), kind=kLoop, calls=%fused_computation.134 | loop fusion | flops 1638400 | bytes 1966081 | tf_op jit(solution)/shard_map/convert_element_type | solution.py:56
  46.6 2.2 %collective-permute-start.3 = (bf16[1,8,16,640]{3,2,1,0:T(8,128)(2,1)S(1)}, bf16[1,8,16,640]{3,2,1,0:T(8,128)(2,1)S(1)}, u32[]{:S(2)}, u32[]{:S(2)}) collective-permute-start(bf16[1,8,16,640]{3,2,1,0:T(8,128)(2,1)S(1)} %get-tuple-element.37), channel_id=1, source_target_pairs={{0,1},{1,2},{2,3},{3,4},{4,5},{5,6},{6,7},{8,9},{9,10},{10,11},{11... | collective-permute-start | bytes 491528 | tf_op jit(solution)/shard_map/ppermute | solution.py:15
  48.9 4.2 %collective-permute-start.4 = (bf16[1,8,16,640]{3,2,1,0:T(8,128)(2,1)S(1)}, bf16[1,8,16,640]{3,2,1,0:T(8,128)(2,1)S(1)}, u32[]{:S(2)}, u32[]{:S(2)}) collective-permute-start(bf16[1,8,16,640]{3,2,1,0:T(8,128)(2,1)S(1)} %get-tuple-element.38), channel_id=1, source_target_pairs={{1,0},{2,1},{3,2},{4,3},{5,4},{6,5},{7,6},{9,8},{10,9},{11,10},{12... | collective-permute-start | bytes 491528 | tf_op jit(solution)/shard_map/ppermute | solution.py:17
  53.5 2.0 %collective-permute-done.3 = bf16[1,8,16,640]{3,2,1,0:T(8,128)(2,1)S(1)} collective-permute-done((bf16[1,8,16,640]{3,2,1,0:T(8,128)(2,1)S(1)}, bf16[1,8,16,640]{3,2,1,0:T(8,128)(2,1)S(1)}, u32[]{:S(2)}, u32[]{:S(2)}) %collective-permute-start.3) | collective-permute-done | bytes 163872 | tf_op jit(solution)/shard_map/ppermute | solution.py:15
  55.5 3.6 %collective-permute-done.4 = bf16[1,8,16,640]{3,2,1,0:T(8,128)(2,1)S(1)} collective-permute-done((bf16[1,8,16,640]{3,2,1,0:T(8,128)(2,1)S(1)}, bf16[1,8,16,640]{3,2,1,0:T(8,128)(2,1)S(1)}, u32[]{:S(2)}, u32[]{:S(2)}) %collective-permute-start.4) | collective-permute-done | bytes 163872 | tf_op jit(solution)/shard_map/ppermute | solution.py:17
  59.6 0.5 fusion.8
  60.2 1.3 %collective-permute-start.5 = (bf16[2,8,16,640]{3,2,1,0:T(8,128)(2,1)S(1)}, bf16[2,8,16,640]{3,2,1,0:T(8,128)(2,1)S(1)}, u32[]{:S(2)}, u32[]{:S(2)}) collective-permute-start(bf16[2,8,16,640]{3,2,1,0:T(8,128)(2,1)S(1)} %fusion.29), channel_id=1, source_target_pairs={{0,8},{1,9},{2,10},{3,11},{4,12},{5,13},{6,14},{7,15},{16,24},{17,... | collective-permute-start | bytes 983048 | tf_op jit(solution)/shard_map/ppermute | solution.py:27
  61.5 2.2 %collective-permute-done.5 = bf16[2,8,16,640]{3,2,1,0:T(8,128)(2,1)S(1)} collective-permute-done((bf16[2,8,16,640]{3,2,1,0:T(8,128)(2,1)S(1)}, bf16[2,8,16,640]{3,2,1,0:T(8,128)(2,1)S(1)}, u32[]{:S(2)}, u32[]{:S(2)}) %collective-permute-start.5) | collective-permute-done | bytes 327712 | tf_op jit(solution)/shard_map/ppermute | solution.py:27
  68.7 2.7 %collective-permute-start.6 = (bf16[1,8,16,640]{3,2,1,0:T(8,128)(2,1)S(1)}, bf16[1,8,16,640]{3,2,1,0:T(8,128)(2,1)S(1)}, u32[]{:S(2)}, u32[]{:S(2)}) collective-permute-start(bf16[1,8,16,640]{3,2,1,0:T(8,128)(2,1)S(1)} %get-tuple-element.25), channel_id=1, source_target_pairs={{0,1},{1,2},{2,3},{3,4},{4,5},{5,6},{6,7},{8,9},{9,10},{10,11},{11... | collective-permute-start | bytes 491528 | tf_op jit(solution)/shard_map/ppermute | solution.py:15
  71.4 3.5 %collective-permute-start.7 = (bf16[1,8,16,640]{3,2,1,0:T(8,128)(2,1)S(1)}, bf16[1,8,16,640]{3,2,1,0:T(8,128)(2,1)S(1)}, u32[]{:S(2)}, u32[]{:S(2)}) collective-permute-start(bf16[1,8,16,640]{3,2,1,0:T(8,128)(2,1)S(1)} %get-tuple-element.26), channel_id=1, source_target_pairs={{1,0},{2,1},{3,2},{4,3},{5,4},{6,5},{7,6},{9,8},{10,9},{11,10},{12... | collective-permute-start | bytes 491528 | tf_op jit(solution)/shard_map/ppermute | solution.py:17
  75.4 1.8 %collective-permute-done.6 = bf16[1,8,16,640]{3,2,1,0:T(8,128)(2,1)S(1)} collective-permute-done((bf16[1,8,16,640]{3,2,1,0:T(8,128)(2,1)S(1)}, bf16[1,8,16,640]{3,2,1,0:T(8,128)(2,1)S(1)}, u32[]{:S(2)}, u32[]{:S(2)}) %collective-permute-start.6) | collective-permute-done | bytes 163872 | tf_op jit(solution)/shard_map/ppermute | solution.py:15
  77.2 4.0 %collective-permute-done.7 = bf16[1,8,16,640]{3,2,1,0:T(8,128)(2,1)S(1)} collective-permute-done((bf16[1,8,16,640]{3,2,1,0:T(8,128)(2,1)S(1)}, bf16[1,8,16,640]{3,2,1,0:T(8,128)(2,1)S(1)}, u32[]{:S(2)}, u32[]{:S(2)}) %collective-permute-start.7) | collective-permute-done | bytes 163872 | tf_op jit(solution)/shard_map/ppermute | solution.py:17
  81.7 0.5 fusion.7
  82.3 1.3 %collective-permute-start.8 = (bf16[2,8,16,640]{3,2,1,0:T(8,128)(2,1)S(1)}, bf16[2,8,16,640]{3,2,1,0:T(8,128)(2,1)S(1)}, u32[]{:S(2)}, u32[]{:S(2)}) collective-permute-start(bf16[2,8,16,640]{3,2,1,0:T(8,128)(2,1)S(1)} %fusion.39), channel_id=1, source_target_pairs={{0,8},{1,9},{2,10},{3,11},{4,12},{5,13},{6,14},{7,15},{16,24},{17,... | collective-permute-start | bytes 983048 | tf_op jit(solution)/shard_map/ppermute | solution.py:27
  83.7 2.1 %collective-permute-done.8 = bf16[2,8,16,640]{3,2,1,0:T(8,128)(2,1)S(1)} collective-permute-done((bf16[2,8,16,640]{3,2,1,0:T(8,128)(2,1)S(1)}, bf16[2,8,16,640]{3,2,1,0:T(8,128)(2,1)S(1)}, u32[]{:S(2)}, u32[]{:S(2)}) %collective-permute-start.8) | collective-permute-done | bytes 327712 | tf_op jit(solution)/shard_map/ppermute | solution.py:27
  90.8 2.1 %collective-permute-start.9 = (bf16[1,8,16,640]{3,2,1,0:T(8,128)(2,1)S(1)}, bf16[1,8,16,640]{3,2,1,0:T(8,128)(2,1)S(1)}, u32[]{:S(2)}, u32[]{:S(2)}) collective-permute-start(bf16[1,8,16,640]{3,2,1,0:T(8,128)(2,1)S(1)} %get-tuple-element.13), channel_id=1, source_target_pairs={{0,1},{1,2},{2,3},{3,4},{4,5},{5,6},{6,7},{8,9},{9,10},{10,11},{11... | collective-permute-start | bytes 491528 | tf_op jit(solution)/shard_map/ppermute | solution.py:15
  92.9 4.1 %collective-permute-start.10 = (bf16[1,8,16,640]{3,2,1,0:T(8,128)(2,1)S(1)}, bf16[1,8,16,640]{3,2,1,0:T(8,128)(2,1)S(1)}, u32[]{:S(2)}, u32[]{:S(2)}) collective-permute-start(bf16[1,8,16,640]{3,2,1,0:T(8,128)(2,1)S(1)} %get-tuple-element.14), channel_id=1, source_target_pairs={{1,0},{2,1},{3,2},{4,3},{5,4},{6,5},{7,6},{9,8},{10,9},{11,10},{12... | collective-permute-start | bytes 491528 | tf_op jit(solution)/shard_map/ppermute | solution.py:17
  97.4 1.8 %collective-permute-done.9 = bf16[1,8,16,640]{3,2,1,0:T(8,128)(2,1)S(1)} collective-permute-done((bf16[1,8,16,640]{3,2,1,0:T(8,128)(2,1)S(1)}, bf16[1,8,16,640]{3,2,1,0:T(8,128)(2,1)S(1)}, u32[]{:S(2)}, u32[]{:S(2)}) %collective-permute-start.9) | collective-permute-done | bytes 163872 | tf_op jit(solution)/shard_map/ppermute | solution.py:15
  99.2 4.0 %collective-permute-done.10 = bf16[1,8,16,640]{3,2,1,0:T(8,128)(2,1)S(1)} collective-permute-done((bf16[1,8,16,640]{3,2,1,0:T(8,128)(2,1)S(1)}, bf16[1,8,16,640]{3,2,1,0:T(8,128)(2,1)S(1)}, u32[]{:S(2)}, u32[]{:S(2)}) %collective-permute-start.10) | collective-permute-done | bytes 163872 | tf_op jit(solution)/shard_map/ppermute | solution.py:17
  103.8 0.5 fusion.6
  104.3 1.3 %maximum_bitcast_fusion = bf16[1,4,2,8,16,640]{5,4,3,2,1,0:T(8,128)(2,1)} fusion(bf16[1,2,8,16,640]{4,3,2,1,0:T(8,128)(2,1)S(1)} %fusion.74, bf16[1,2,8,16,640]{4,3,2,1,0:T(8,128)(2,1)S(1)} %bitcast.271, bf16[1,2,8,16,640]{4,3,2,1,0:T(8,128)(2,1)S(1)} %bitcast.270, bf16[1,2,8,16,640]{4,3,2,1,0:T(8,128)(2,1)S(1)} %add_convert_fusion), kind=kLoop, calls=%fused_computation.4 | loop fusion | flops 1966080 | bytes 2621440 | tf_op jit(solution)/shard_map/broadcast_in_dim | solution.py:82
  (90 shorter events, 18.1 us)
Async XLA Ops:
  10.8 7.5 %copy-start = (bf16[9,640,640]{2,1,0:T(8,128)(2,1)}, bf16[9,640,640]{2,1,0:T(8,128)(2,1)S(1)}, u32[]{:S(2)}) copy-start(bf16[9,640,640]{2,1,0:T(8,128)(2,1)S(1)} %fusion) | copy-start | bytes 22118404
  10.8 6.0 %copy-start.13 = (bf16[2,8,16,640]{3,2,1,0:T(8,128)(2,1)S(1)}, bf16[2,8,16,640]{3,2,1,0:T(8,128)(2,1)}, u32[]{:S(2)}) copy-start(bf16[2,8,16,640]{3,2,1,0:T(8,128)(2,1)} %get-tuple-element.55) | copy-start | bytes 983044
  10.8 6.5 %copy-start.12 = (bf16[2,8,16,640]{3,2,1,0:T(8,128)(2,1)S(1)}, bf16[2,8,16,640]{3,2,1,0:T(8,128)(2,1)}, u32[]{:S(2)}) copy-start(bf16[2,8,16,640]{3,2,1,0:T(8,128)(2,1)} %get-tuple-element.56) | copy-start | bytes 983044
  12.6 5.2 %copy-start.11 = (bf16[2,8,16,640]{3,2,1,0:T(8,128)(2,1)S(1)}, bf16[2,8,16,640]{3,2,1,0:T(8,128)(2,1)}, u32[]{:S(2)}) copy-start(bf16[2,8,16,640]{3,2,1,0:T(8,128)(2,1)} %get-tuple-element.57) | copy-start | bytes 983044
  13.1 5.2 %copy-start.3 = (bf16[1,2,8,16,640]{4,3,2,1,0:T(8,128)(2,1)S(1)}, bf16[1,2,8,16,640]{4,3,2,1,0:T(8,128)(2,1)}, u32[]{:S(2)}) copy-start(bf16[1,2,8,16,640]{4,3,2,1,0:T(8,128)(2,1)} %param.6) | copy-start | bytes 983044
  13.1 5.2 %copy-start.10 = (bf16[2,8,16,640]{3,2,1,0:T(8,128)(2,1)S(1)}, bf16[2,8,16,640]{3,2,1,0:T(8,128)(2,1)}, u32[]{:S(2)}) copy-start(bf16[2,8,16,640]{3,2,1,0:T(8,128)(2,1)} %get-tuple-element.51) | copy-start | bytes 983044
  16.3 8.9 %copy-start.14 = (f32[1,5,640]{2,0,1:T(1,128)S(1)}, f32[1,5,640]{2,0,1:T(1,128)}, u32[]{:S(2)}) copy-start(f32[1,5,640]{2,0,1:T(1,128)} %param.11) | copy-start | bytes 38404
  16.8 8.5 %copy-start.9 = (bf16[1,3,640,640]{3,2,1,0:T(8,128)(2,1)S(1)}, bf16[1,3,640,640]{3,2,1,0:T(8,128)(2,1)}, u32[]{:S(2)}) copy-start(bf16[1,3,640,640]{3,2,1,0:T(8,128)(2,1)} %param.10) | copy-start | bytes 7372804
  18.8 13.7 %copy-start.4 = (f32[256,640]{1,0:T(8,128)}, f32[256,640]{1,0:T(8,128)S(1)}, u32[]{:S(2)}) copy-start(f32[256,640]{1,0:T(8,128)S(1)} %get-tuple-element.60) | copy-start | bytes 1966084
  19.0 7.9 %collective-permute-start = (bf16[1,8,16,640]{3,2,1,0:T(8,128)(2,1)S(1)}, bf16[1,8,16,640]{3,2,1,0:T(8,128)(2,1)S(1)}, u32[]{:S(2)}, u32[]{:S(2)}) collective-permute-start(bf16[1,8,16,640]{3,2,1,0:T(8,128)(2,1)S(1)} %get-tuple-element.49), channel_id=1, source_target_pairs={{0,1},{1,2},{2,3},{3,4},{4,5},{5,6},{6,7},{8,9},{9,10},{10,11},{11... | collective-permute-start | bytes 491528 | tf_op jit(solution)/shard_map/ppermute | solution.py:15
  22.2 9.3 %collective-permute-start.1 = (bf16[1,8,16,640]{3,2,1,0:T(8,128)(2,1)S(1)}, bf16[1,8,16,640]{3,2,1,0:T(8,128)(2,1)S(1)}, u32[]{:S(2)}, u32[]{:S(2)}) collective-permute-start(bf16[1,8,16,640]{3,2,1,0:T(8,128)(2,1)S(1)} %get-tuple-element.50), channel_id=1, source_target_pairs={{1,0},{2,1},{3,2},{4,3},{5,4},{6,5},{7,6},{9,8},{10,9},{11,10},{12... | collective-permute-start | bytes 491528 | tf_op jit(solution)/shard_map/ppermute | solution.py:17
  25.9 6.1 %copy-start.1 = (bf16[3,640,640]{2,1,0:T(8,128)(2,1)}, bf16[3,640,640]{2,1,0:T(8,128)(2,1)S(1)}, u32[]{:S(2)}) copy-start(bf16[3,640,640]{2,1,0:T(8,128)(2,1)S(1)} %fusion.1) | copy-start | bytes 7372804
  31.5 10.5 %slice-start = ((s8[7372800]{0:T(1024)(128)(4,1)}), s8[3178496]{0:T(1024)(128)(4,1)S(1)}, s32[]{:S(2)}) async-start(s8[7372800]{0:T(1024)(128)(4,1)} %bitcast.246), calls=%async_computation | async-start | bytes 6356992
  32.5 0.9 copy-start.6
  33.4 3.9 %collective-permute-start.2 = (bf16[2,8,16,640]{3,2,1,0:T(8,128)(2,1)}, bf16[2,8,16,640]{3,2,1,0:T(8,128)(2,1)}, u32[]{:S(2)}, u32[]{:S(2)}) collective-permute-start(bf16[2,8,16,640]{3,2,1,0:T(8,128)(2,1)} %fusion.19), channel_id=1, source_target_pairs={{0,8},{1,9},{2,10},{3,11},{4,12},{5,13},{6,14},{7,15},{16,24},{17,... | collective-permute-start | bytes 983048 | tf_op jit(solution)/shard_map/ppermute | solution.py:27
  34.7 7.3 %slice-start.1 = ((s8[7372800]{0:T(1024)(128)(4,1)}), s8[4194304]{0:T(1024)(128)(4,1)S(1)}, s32[]{:S(2)}) async-start(s8[7372800]{0:T(1024)(128)(4,1)} %bitcast.246), calls=%async_computation.1 | async-start | bytes 8388608
  42.5 2.8 %copy-start.8 = (bf16[3,2,8,16,640]{4,3,2,1,0:T(8,128)(2,1)S(1)}, bf16[3,2,8,16,640]{4,3,2,1,0:T(8,128)(2,1)}, u32[]{:S(2)}) copy-start(bf16[3,2,8,16,640]{4,3,2,1,0:T(8,128)(2,1)} %param.7) | copy-start | bytes 2949124
  43.0 10.0 %copy-start.2 = (bf16[3,640,640]{2,1,0:T(8,128)(2,1)S(1)}, bf16[3,640,640]{2,1,0:T(8,128)(2,1)}, u32[]{:S(2)}) copy-start(bf16[3,640,640]{2,1,0:T(8,128)(2,1)} %copy-done.1) | copy-start | bytes 7372804
  46.6 8.9 %collective-permute-start.3 = (bf16[1,8,16,640]{3,2,1,0:T(8,128)(2,1)S(1)}, bf16[1,8,16,640]{3,2,1,0:T(8,128)(2,1)S(1)}, u32[]{:S(2)}, u32[]{:S(2)}) collective-permute-start(bf16[1,8,16,640]{3,2,1,0:T(8,128)(2,1)S(1)} %get-tuple-element.37), channel_id=1, source_target_pairs={{0,1},{1,2},{2,3},{3,4},{4,5},{5,6},{6,7},{8,9},{9,10},{10,11},{11... | collective-permute-start | bytes 491528 | tf_op jit(solution)/shard_map/ppermute | solution.py:15
  48.9 10.2 %collective-permute-start.4 = (bf16[1,8,16,640]{3,2,1,0:T(8,128)(2,1)S(1)}, bf16[1,8,16,640]{3,2,1,0:T(8,128)(2,1)S(1)}, u32[]{:S(2)}, u32[]{:S(2)}) collective-permute-start(bf16[1,8,16,640]{3,2,1,0:T(8,128)(2,1)S(1)} %get-tuple-element.38), channel_id=1, source_target_pairs={{1,0},{2,1},{3,2},{4,3},{5,4},{6,5},{7,6},{9,8},{10,9},{11,10},{12... | collective-permute-start | bytes 491528 | tf_op jit(solution)/shard_map/ppermute | solution.py:17
  60.2 3.5 %collective-permute-start.5 = (bf16[2,8,16,640]{3,2,1,0:T(8,128)(2,1)S(1)}, bf16[2,8,16,640]{3,2,1,0:T(8,128)(2,1)S(1)}, u32[]{:S(2)}, u32[]{:S(2)}) collective-permute-start(bf16[2,8,16,640]{3,2,1,0:T(8,128)(2,1)S(1)} %fusion.29), channel_id=1, source_target_pairs={{0,8},{1,9},{2,10},{3,11},{4,12},{5,13},{6,14},{7,15},{16,24},{17,... | collective-permute-start | bytes 983048 | tf_op jit(solution)/shard_map/ppermute | solution.py:27
  67.9 15.6 %copy-start.5 = (f32[256,640]{1,0:T(8,128)S(1)}, f32[256,640]{1,0:T(8,128)}, u32[]{:S(2)}) copy-start(f32[256,640]{1,0:T(8,128)} %copy-done.4) | copy-start | bytes 1966084
  67.9 15.6 %copy-start.7 = (f32[256,640]{1,0:T(8,128)S(1)}, f32[256,640]{1,0:T(8,128)}, u32[]{:S(2)}) copy-start(f32[256,640]{1,0:T(8,128)} %copy-done.6) | copy-start | bytes 1966084
  68.7 8.5 %collective-permute-start.6 = (bf16[1,8,16,640]{3,2,1,0:T(8,128)(2,1)S(1)}, bf16[1,8,16,640]{3,2,1,0:T(8,128)(2,1)S(1)}, u32[]{:S(2)}, u32[]{:S(2)}) collective-permute-start(bf16[1,8,16,640]{3,2,1,0:T(8,128)(2,1)S(1)} %get-tuple-element.25), channel_id=1, source_target_pairs={{0,1},{1,2},{2,3},{3,4},{4,5},{5,6},{6,7},{8,9},{9,10},{10,11},{11... | collective-permute-start | bytes 491528 | tf_op jit(solution)/shard_map/ppermute | solution.py:15
  71.4 9.8 %collective-permute-start.7 = (bf16[1,8,16,640]{3,2,1,0:T(8,128)(2,1)S(1)}, bf16[1,8,16,640]{3,2,1,0:T(8,128)(2,1)S(1)}, u32[]{:S(2)}, u32[]{:S(2)}) collective-permute-start(bf16[1,8,16,640]{3,2,1,0:T(8,128)(2,1)S(1)} %get-tuple-element.26), channel_id=1, source_target_pairs={{1,0},{2,1},{3,2},{4,3},{5,4},{6,5},{7,6},{9,8},{10,9},{11,10},{12... | collective-permute-start | bytes 491528 | tf_op jit(solution)/shard_map/ppermute | solution.py:17
  82.3 3.5 %collective-permute-start.8 = (bf16[2,8,16,640]{3,2,1,0:T(8,128)(2,1)S(1)}, bf16[2,8,16,640]{3,2,1,0:T(8,128)(2,1)S(1)}, u32[]{:S(2)}, u32[]{:S(2)}) collective-permute-start(bf16[2,8,16,640]{3,2,1,0:T(8,128)(2,1)S(1)} %fusion.39), channel_id=1, source_target_pairs={{0,8},{1,9},{2,10},{3,11},{4,12},{5,13},{6,14},{7,15},{16,24},{17,... | collective-permute-start | bytes 983048 | tf_op jit(solution)/shard_map/ppermute | solution.py:27
  90.8 8.5 %collective-permute-start.9 = (bf16[1,8,16,640]{3,2,1,0:T(8,128)(2,1)S(1)}, bf16[1,8,16,640]{3,2,1,0:T(8,128)(2,1)S(1)}, u32[]{:S(2)}, u32[]{:S(2)}) collective-permute-start(bf16[1,8,16,640]{3,2,1,0:T(8,128)(2,1)S(1)} %get-tuple-element.13), channel_id=1, source_target_pairs={{0,1},{1,2},{2,3},{3,4},{4,5},{5,6},{6,7},{8,9},{9,10},{10,11},{11... | collective-permute-start | bytes 491528 | tf_op jit(solution)/shard_map/ppermute | solution.py:15
  92.9 10.3 %collective-permute-start.10 = (bf16[1,8,16,640]{3,2,1,0:T(8,128)(2,1)S(1)}, bf16[1,8,16,640]{3,2,1,0:T(8,128)(2,1)S(1)}, u32[]{:S(2)}, u32[]{:S(2)}) collective-permute-start(bf16[1,8,16,640]{3,2,1,0:T(8,128)(2,1)S(1)} %get-tuple-element.14), channel_id=1, source_target_pairs={{1,0},{2,1},{3,2},{4,3},{5,4},{6,5},{7,6},{9,8},{10,9},{11,10},{12... | collective-permute-start | bytes 491528 | tf_op jit(solution)/shard_map/ppermute | solution.py:17
where the time goes:
time: 106 us
  waiting for transfers between devices  29.1 us (27%)
  starting transfers between devices  28.8 us (27%)
  matrix products  28.1 us (27%)
  other arithmetic  14.2 us (13%)
  local copies, waits for them, and re-layouts  4.6 us (4%)
    dot_general x36, matrix products, spatial_term(): jnp.dot(window, kernels[row_tap * 3 + col_tap], preferred_element_type=jn...  22.5 us
    ppermute x4, waiting for transfers between devices, with_halo(): lax.ppermute(head, axis, [((i + 1) % count, i) for i in range(ends)])  16.1 us
    ppermute x4, starting transfers between devices, with_halo(): lax.ppermute(head, axis, [((i + 1) % count, i) for i in range(ends)])  14.8 us
    ppermute x4, starting transfers between devices, with_halo(): lax.ppermute(tail, axis, [(i, (i + 1) % count) for i in range(ends)])  10.1 us
    ppermute x3, waiting for transfers between devices, passed_along(): lax.ppermute(value, axis, [(source, source + steps) for source in range(i...  6.87 us
    ppermute x4, waiting for transfers between devices, with_halo(): lax.ppermute(tail, axis, [(i, (i + 1) % count) for i in range(ends)])  6.06 us
    dot_general x12, matrix products, section_local(): jnp.dot(window, temporal_kernels[frame_tap], preferred_element_type=jnp.f...  5.58 us
    convert_element_type x2, other arithmetic, dequantize(): return (weights.astype(jnp.float32) * expanded[None]).astype(jnp.bfloat16)  5.49 us
  transfers between devices with their start and end apart: 11, of which 11 were waited for; matrix products, arithmetic and copies ran while one was open for 2% of the time, Pallas kernels for 0%

commit v1 on v0

v1 whole, which is shorter than its diff:
```python
import functools

import jax
import jax.numpy as jnp
from jax import lax
from jax.experimental import pallas as pl
from jax.experimental.pallas import tpu as pltpu
from jax.sharding import PartitionSpec as P

MESH = pl.DeviceIdType.MESH


def silu(v):
    return v / (1.0 + jnp.exp(-v))


def kernel(
    n_segment, n_seq,
    held, arrivals, w_s, s_s, w_t, s_t, out,
    clips, padded, ks, kt, middle, ext, results,
    clip_sem, ks_sem, kt_sem, out_sem, relay_send, relay_recv, halo_send, halo_recv,
):
    ticks, frames, height, width, channels = clips.shape
    rows = frames * height * width
    segment, seq = lax.axis_index("segment"), lax.axis_index("seq")
    has_left, has_right = seq > 0, seq < n_seq - 1
    has_up, has_down = segment > 0, segment < n_segment - 1
    neighbours = (
        (has_left, {"seq": seq - 1}),
        (has_right, {"seq": seq + 1}),
        (has_up, {"segment": segment - 1}),
        (has_down, {"segment": segment + 1}),
    )
    barrier = pltpu.get_barrier_semaphore()
    for there, where in neighbours:
        @pl.when(there)
        def _(where=where):
            pl.semaphore_signal(barrier, inc=1, device_id=where, device_id_type=MESH)

    def load_held():
        return pltpu.make_async_copy(held.at[0], clips.at[0], clip_sem.at[0])

    def load_arrival(t):
        return pltpu.make_async_copy(arrivals.at[t - 1], clips.at[t], clip_sem.at[t])

    def load_ks(row):
        return pltpu.make_async_copy(w_s.at[0, pl.ds(3 * row, 3)], ks.at[pl.ds(3 * row, 3)], ks_sem.at[row])

    def load_kt():
        return pltpu.make_async_copy(w_t.at[0], kt, kt_sem)

    def store(t):
        return pltpu.make_async_copy(results.at[t], out.at[0, t], out_sem.at[t])

    def relay(t):
        return pltpu.make_async_remote_copy(
            results.at[t], clips.at[t + 1], relay_send.at[t], relay_recv.at[t],
            device_id={"segment": segment + 1}, device_id_type=MESH,
        )

    def tail(t):
        return pltpu.make_async_remote_copy(
            ext.at[t, frames], ext.at[t, 0], halo_send.at[t, 0], halo_recv.at[t, 0],
            device_id={"seq": seq + 1}, device_id_type=MESH,
        )

    def head(t):
        return pltpu.make_async_remote_copy(
            ext.at[t, 1], ext.at[t, frames + 1], halo_send.at[t, 1], halo_recv.at[t, 1],
            device_id={"seq": seq - 1}, device_id_type=MESH,
        )

    load_held().start()
    for row in range(3):
        load_ks(row).start()
    load_kt().start()

    @pl.when(segment == 0)
    def _():
        for t in range(1, ticks):
            load_arrival(t).start()

    blank = jnp.zeros((frames, 1, width, 3 * channels), jnp.bfloat16)
    padded[:, 0:1] = blank
    padded[:, height + 1 : height + 2] = blank

    @pl.when(jnp.logical_not(has_left))
    def _():
        ext[:, 0] = jnp.zeros((ticks, height, width, channels), jnp.bfloat16)

    @pl.when(jnp.logical_not(has_right))
    def _():
        ext[:, frames + 1] = jnp.zeros((ticks, height, width, channels), jnp.bfloat16)

    def scale(kernels, tap, scales):
        blocks = scales.shape[1]
        block = channels // blocks
        for i in range(blocks):
            part = slice(i * block, (i + 1) * block)
            kernels[tap, part, :] = (
                kernels[tap, part, :].astype(jnp.float32) * scales[0, i : i + 1, :]
            ).astype(jnp.bfloat16)

    def spatial(t, first):
        x = clips[t].reshape(rows, channels).astype(jnp.float32)
        lifted = silu(x)
        column = lax.broadcasted_iota(jnp.int32, (rows, channels), 0) % width
        before = jnp.where(column == 0, 0.0, pltpu.roll(lifted, 1, 0))
        after = jnp.where(column == width - 1, 0.0, pltpu.roll(lifted, rows - 1, 0))
        for b, part in enumerate((before, lifted, after)):
            padded[:, 1 : height + 1, :, b * channels : (b + 1) * channels] = part.astype(
                jnp.bfloat16
            ).reshape(frames, height, width, channels)
        total = x
        for a in range(3):
            if first:
                load_ks(a).wait()
                for b in range(3):
                    scale(ks, 3 * a + b, s_s)
            total = total + jnp.dot(
                padded[:, a : a + height].reshape(rows, 3 * channels),
                ks[3 * a : 3 * a + 3].reshape(3 * channels, channels),
                preferred_element_type=jnp.float32,
            )
        mid = total.astype(jnp.bfloat16)
        middle[t] = mid
        ext[t, 1 : frames + 1] = silu(mid.astype(jnp.float32)).astype(jnp.bfloat16).reshape(
            frames, height, width, channels
        )

    def send_halo(t):
        @pl.when(has_right)
        def _():
            tail(t).start()

        @pl.when(has_left)
        def _():
            head(t).start()

    def temporal(t):
        @pl.when(has_left)
        def _():
            tail(t).wait_recv()

        @pl.when(has_right)
        def _():
            head(t).wait_recv()

        total = jnp.zeros((rows, channels), jnp.float32)
        for j in range(3):
            total = total + jnp.dot(
                ext[t, j : j + frames].reshape(rows, channels), kt[j],
                preferred_element_type=jnp.float32,
            )
        results[t] = (
            middle[t].astype(jnp.float32) + total.astype(jnp.bfloat16).astype(jnp.float32)
        ).astype(jnp.bfloat16).reshape(frames, height, width, channels)
        store(t).start()

    load_held().wait()
    spatial(0, True)
    pl.semaphore_wait(barrier, sum(there.astype(jnp.int32) for there, _ in neighbours))
    send_halo(0)
    load_kt().wait()
    for j in range(3):
        scale(kt, j, s_t)

    def step(t, carry):
        @pl.when(segment == 0)
        def _():
            load_arrival(t).wait()

        @pl.when(has_up)
        def _():
            relay(t - 1).wait_recv()

        spatial(t, False)
        send_halo(t)
        temporal(t - 1)

        @pl.when(has_down)
        def _():
            relay(t - 1).start()

        return carry

    lax.fori_loop(1, ticks, step, 0)
    temporal(ticks - 1)

    for t in range(ticks):
        store(t).wait()

        @pl.when(has_right)
        def _(t=t):
            tail(t).wait_send()

        @pl.when(has_left)
        def _(t=t):
            head(t).wait_send()

        if t < ticks - 1:
            @pl.when(has_down)
            def _(t=t):
                relay(t).wait_send()


def local(n_segment, n_seq, held, arrivals, w_s, s_s, w_t, s_t):
    ticks = arrivals.shape[0] + 1
    _, frames, height, width, channels = held.shape
    clip = (frames, height, width, channels)
    bf16, dma = jnp.bfloat16, pltpu.SemaphoreType.DMA
    hbm, vmem = pl.BlockSpec(memory_space=pl.ANY), pl.BlockSpec(memory_space=pltpu.VMEM)
    rows = frames * height * width
    return pl.pallas_call(
        functools.partial(kernel, n_segment, n_seq),
        out_shape=jax.ShapeDtypeStruct((1, ticks) + clip, bf16),
        in_specs=[hbm, hbm, hbm, vmem, hbm, vmem],
        out_specs=hbm,
        scratch_shapes=[
            pltpu.VMEM((ticks,) + clip, bf16),
            pltpu.VMEM((frames, height + 2, width, 3 * channels), bf16),
            pltpu.VMEM(w_s.shape[1:], bf16),
            pltpu.VMEM(w_t.shape[1:], bf16),
            pltpu.VMEM((ticks, rows, channels), bf16),
            pltpu.VMEM((ticks, frames + 2, height, width, channels), bf16),
            pltpu.VMEM((ticks,) + clip, bf16),
            dma((ticks,)), dma((3,)), dma, dma((ticks,)),
            dma((ticks,)), dma((ticks,)), dma((ticks, 2)), dma((ticks, 2)),
        ],
        compiler_params=pltpu.CompilerParams(
            collective_id=0, has_side_effects=True, vmem_limit_bytes=48 * 2**20
        ),
        cost_estimate=pl.CostEstimate(
            flops=2 * ticks * 12 * rows * channels * channels, bytes_accessed=2 * (w_s.size + w_t.size),
            transcendentals=0,
        ),
    )(held, arrivals, w_s, s_s, w_t, s_t)


def solution(mesh):
    in_specs = (
        P("segment", ("groups", "seq"), None, None, None),
        P(None, ("groups", "seq"), None, None, None),
        P("segment", None, None, None),
        P("segment", None, None),
        P("segment", None, None, None),
        P("segment", None, None),
    )
    out_specs = P("segment", None, ("groups", "seq"), None, None, None)
    body = functools.partial(local, mesh.shape["segment"], mesh.shape["seq"])
    return jax.shard_map(body, mesh=mesh, in_specs=in_specs, out_specs=out_specs, check_vma=False)
```

time: 106 us -> 51.4 us (0.48)
  Pallas kernels: 0 us -> 44.7 us
  waiting for transfers between devices: 29.1 us -> 0 us
  starting transfers between devices: 28.8 us -> 0 us
  matrix products: 28.1 us -> 0 us
  other arithmetic: 14.2 us -> 0 us
  local copies, waits for them, and re-layouts: 4.6 us -> 6.35 us
    pallas_call x0 -> x1, Pallas kernels: none -> 44.7 us  [local(): pl.pallas_call(functools.partial(kernel, n_segment, n_seq), out_shape=jax...]
    ppermute x11 -> x0, waiting for transfers between devices: 29.1 us -> none  [the longest x4 16.1 us: with_halo(): lax.ppermute(head, axis, [((i + 1) % count, i) for i in range(ends)])]
    ppermute x11 -> x0, starting transfers between devices: 28.8 us -> none  [the longest x4 14.8 us: with_halo(): lax.ppermute(head, axis, [((i + 1) % count, i) for i in range(ends)])]
    dot_general x48 -> x0, matrix products: 28.1 us -> none  [the longest x36 22.5 us: spatial_term(): jnp.dot(window, kernels[row_tap * 3 + col_tap], preferred_element_type=jn...]
    convert_element_type x15 -> x0, other arithmetic: 12.6 us -> none  [the longest x2 5.49 us: dequantize(): return (weights.astype(jnp.float32) * expanded[None]).astype(jnp.bfloat16)]
    unnamed x36 -> x9, local copies, waits for them, and re-layouts: 0.81 us -> 6.35 us
    slice x8 -> x0, local copies, waits for them, and re-layouts: 2.38 us -> none  [the longest x4 2.26 us: spatial_term(): padded[:, row_tap:row_tap + height, col_tap:col_tap + width]]
    broadcast_in_dim x2 -> x0, local copies, waits for them, and re-layouts: 1.42 us -> none  [dequantize(): expanded = jnp.repeat(scales, block, axis=0)]
  transfers between devices with their start and end apart: 11 -> 0, of which waited for: 11 -> 0; matrix products, arithmetic and copies ran while one was open for 2% -> 0% of each run, Pallas kernels for 0% -> 0%
where the time goes in v1:
time: 51.4 us; the launch traced here: 51.1 us
  Pallas kernels  44.7 us (87%)
  local copies, waits for them, and re-layouts  6.35 us (12%)
    pallas_call x1, Pallas kernels, local(): pl.pallas_call(functools.partial(kernel, n_segment, n_seq), out_shape=jax...  44.7 us
    unnamed x9, local copies, waits for them, and re-layouts  6.35 us

profile of v1, /device:TPU:17, one launch (start us, length us, event | category | flops | bytes accessed | tf_op | source)
XLA Modules:
  0.0 51.1 jit_solution(2261960566788466622)
XLA Ops:
  0.0 0.7 %copy.7.s_s = f32[1,5,640]{2,1,0:T(8,128)S(1)} copy(f32[1,5,640]{2,0,1:T(1,128)} %param.9) | data formatting | bytes 25600 | tf_op args[3]
  0.7 0.7 %copy.8.s_t = f32[1,5,640]{2,1,0:T(8,128)S(1)} copy(f32[1,5,640]{2,0,1:T(1,128)} %param.11) | data formatting | bytes 25600 | tf_op args[5]
  1.4 0.0 copy-start
  1.4 1.7 %copy-done = bf16[1,3,640,640]{3,2,1,0:T(8,128)(2,1)S(1)} copy-done((bf16[1,3,640,640]{3,2,1,0:T(8,128)(2,1)S(1)}, bf16[1,3,640,640]{3,2,1,0:T(8,128)(2,1)}, u32[]{:S(2)}) %copy-start) | copy-done | bytes 2457624
  3.1 0.0 copy-start.1
  3.1 1.2 %copy-done.1 = bf16[3,2,8,16,640]{4,3,2,1,0:T(8,128)(2,1)S(1)} copy-done((bf16[3,2,8,16,640]{4,3,2,1,0:T(8,128)(2,1)S(1)}, bf16[3,2,8,16,640]{4,3,2,1,0:T(8,128)(2,1)}, u32[]{:S(2)}) %copy-start.1) | copy-done | bytes 983064
  4.3 0.0 copy-start.2
  4.3 1.0 %copy-done.2 = bf16[1,2,8,16,640]{4,3,2,1,0:T(8,128)(2,1)S(1)} copy-done((bf16[1,2,8,16,640]{4,3,2,1,0:T(8,128)(2,1)S(1)}, bf16[1,2,8,16,640]{4,3,2,1,0:T(8,128)(2,1)}, u32[]{:S(2)}) %copy-start.2) | copy-done | bytes 327704
  5.3 44.7 %shard_map.64 = bf16[1,4,2,8,16,640]{5,4,3,2,1,0:T(8,128)(2,1)S(1)} custom-call(bf16[1,2,8,16,640]{4,3,2,1,0:T(8,128)(2,1)S(1)} %copy-done.2, bf16[3,2,8,16,640]{4,3,2,1,0:T(8,128)(2,1)S(1)} %copy-done.1, bf16[1,9,640,640]{3,2,1,0:T(8,128)(2,1)} %w_s.1, f32[1,5,640]{2,1,0:T(8,128)S(1)} %copy.7.s_s, bf16[1,3,640,640]{3,2,1,0:T(8,128)(2,1)S(1)} %copy-done, ...), custom_call_target="tpu_custom_call" | custom-call | flops 10066329600 | bytes 9830400 | tf_op jit(solution)/shard_map/pallas_call | solution.py:214
  50.0 1.1 %copy.10 = bf16[1,4,2,8,16,640]{5,4,3,2,1,0:T(8,128)(2,1)} copy(bf16[1,4,2,8,16,640]{5,4,3,2,1,0:T(8,128)(2,1)S(1)} %shard_map.64) | data formatting | bytes 2621440
Async XLA Ops:
  1.4 1.7 %copy-start = (bf16[1,3,640,640]{3,2,1,0:T(8,128)(2,1)S(1)}, bf16[1,3,640,640]{3,2,1,0:T(8,128)(2,1)}, u32[]{:S(2)}) copy-start(bf16[1,3,640,640]{3,2,1,0:T(8,128)(2,1)} %w_t.1) | copy-start | bytes 7372804
  3.1 1.2 %copy-start.1 = (bf16[3,2,8,16,640]{4,3,2,1,0:T(8,128)(2,1)S(1)}, bf16[3,2,8,16,640]{4,3,2,1,0:T(8,128)(2,1)}, u32[]{:S(2)}) copy-start(bf16[3,2,8,16,640]{4,3,2,1,0:T(8,128)(2,1)} %arrivals.1) | copy-start | bytes 2949124
  4.3 1.0 %copy-start.2 = (bf16[1,2,8,16,640]{4,3,2,1,0:T(8,128)(2,1)S(1)}, bf16[1,2,8,16,640]{4,3,2,1,0:T(8,128)(2,1)}, u32[]{:S(2)}) copy-start(bf16[1,2,8,16,640]{4,3,2,1,0:T(8,128)(2,1)} %held.1) | copy-start | bytes 983044

commit v2 on v1

--- a/solution.py
+++ b/solution.py
@@ -93,12 +93,12 @@
         ext[:, frames + 1] = jnp.zeros((ticks, height, width, channels), jnp.bfloat16)
 
     def scale(kernels, tap, scales):
-        blocks = scales.shape[1]
+        blocks = scales.shape[0]
         block = channels // blocks
         for i in range(blocks):
             part = slice(i * block, (i + 1) * block)
             kernels[tap, part, :] = (
-                kernels[tap, part, :].astype(jnp.float32) * scales[0, i : i + 1, :]
+                kernels[tap, part, :].astype(jnp.float32) * scales[i]
             ).astype(jnp.bfloat16)
 
     def spatial(t, first):
@@ -160,7 +160,11 @@
     load_held().wait()
     spatial(0, True)
     pl.semaphore_wait(barrier, sum(there.astype(jnp.int32) for there, _ in neighbours))
-    send_halo(0)
+
+    @pl.when(segment == 0)
+    def _():
+        send_halo(0)
+
     load_kt().wait()
     for j in range(3):
         scale(kt, j, s_t)
@@ -173,6 +177,10 @@
         @pl.when(has_up)
         def _():
             relay(t - 1).wait_recv()
+
+            @pl.when(t == 1)
+            def _():
+                send_halo(0)
 
         spatial(t, False)
         send_halo(t)
@@ -228,13 +236,13 @@
             dma((ticks,)), dma((ticks,)), dma((ticks, 2)), dma((ticks, 2)),
         ],
         compiler_params=pltpu.CompilerParams(
-            collective_id=0, has_side_effects=True, vmem_limit_bytes=48 * 2**20
+            collective_id=0, has_side_effects=True, vmem_limit_bytes=60 * 2**20
         ),
         cost_estimate=pl.CostEstimate(
             flops=2 * ticks * 12 * rows * channels * channels, bytes_accessed=2 * (w_s.size + w_t.size),
             transcendentals=0,
         ),
-    )(held, arrivals, w_s, s_s, w_t, s_t)
+    )(held, arrivals, w_s, jnp.swapaxes(s_s, 0, 1), w_t, jnp.swapaxes(s_t, 0, 1))
 
 
 def solution(mesh):

time: 51.4 us -> 45.7 us (0.89)
  local copies, waits for them, and re-layouts: 6.35 us -> 2.5 us
  Pallas kernels: 44.7 us -> 42.9 us
    unnamed x9 -> x1, local copies, waits for them, and re-layouts: 6.35 us -> 2.5 us
    pallas_call x1, Pallas kernels: 44.7 us -> 42.9 us  [local(): pl.pallas_call(functools.partial(kernel, n_segment, n_seq), out_shape=jax...]
where the time goes in v2:
time: 45.7 us; the launch traced here: 45.4 us
  Pallas kernels  42.9 us (94%)
  local copies, waits for them, and re-layouts  2.5 us (5%)
    pallas_call x1, Pallas kernels, local(): pl.pallas_call(functools.partial(kernel, n_segment, n_seq), out_shape=jax...  42.9 us
    unnamed x1, local copies, waits for them, and re-layouts  2.5 us

profile of v2, /device:TPU:17, one launch (start us, length us, event | category | flops | bytes accessed | tf_op | source)
XLA Modules:
  0.0 45.4 jit_solution(16968912307253211057)
XLA Ops:
  0.0 42.9 %shard_map.64 = bf16[1,4,2,8,16,640]{5,4,3,2,1,0:T(8,128)(2,1)} custom-call(bf16[1,2,8,16,640]{4,3,2,1,0:T(8,128)(2,1)} %held.1, bf16[3,2,8,16,640]{4,3,2,1,0:T(8,128)(2,1)} %arrivals.1, bf16[1,9,640,640]{3,2,1,0:T(8,128)(2,1)} %w_s.1, f32[5,1,640]{2,1,0:T(1,128)} %bitcast.2, bf16[1,3,640,640]{3,2,1,0:T(8,128)(2,1)} %w_t.1, f32[5,1,640]{2,1,0:T(1,128)} %bitcast.3), custom_call_target="tpu_custom_call" | custom-call | flops 10066329600 | bytes 9830400 | tf_op jit(solution)/shard_map/pallas_call | solution.py:222
  42.9 2.5 %copy.8 = bf16[1,4,2,8,16,640]{5,4,3,2,1,0:T(8,128)(2,1)} copy(bf16[1,4,2,8,16,640]{5,4,3,2,1,0:T(8,128)(2,1)} %shard_map.64) | data formatting | bytes 2621440

commit v3 on v2

--- a/solution.py
+++ b/solution.py
@@ -138,20 +138,25 @@
             head(t).start()
 
     def temporal(t):
-        @pl.when(has_left)
-        def _():
-            tail(t).wait_recv()
-
-        @pl.when(has_right)
-        def _():
-            head(t).wait_recv()
-
-        total = jnp.zeros((rows, channels), jnp.float32)
-        for j in range(3):
-            total = total + jnp.dot(
+        def tap(j):
+            return jnp.dot(
                 ext[t, j : j + frames].reshape(rows, channels), kt[j],
                 preferred_element_type=jnp.float32,
             )
+
+        total = tap(1)
+
+        @pl.when(has_left)
+        def _():
+            tail(t).wait_recv()
+
+        total = total + tap(0)
+
+        @pl.when(has_right)
+        def _():
+            head(t).wait_recv()
+
+        total = total + tap(2)
         results[t] = (
             middle[t].astype(jnp.float32) + total.astype(jnp.bfloat16).astype(jnp.float32)
         ).astype(jnp.bfloat16).reshape(frames, height, width, channels)
@@ -183,12 +188,21 @@
                 send_halo(0)
 
         spatial(t, False)
-        send_halo(t)
+        late = (segment == 0) & (t == ticks - 1)
+
+        @pl.when(jnp.logical_not(late))
+        def _():
+            send_halo(t)
+
         temporal(t - 1)
 
         @pl.when(has_down)
         def _():
             relay(t - 1).start()
+
+        @pl.when(late)
+        def _():
+            send_halo(t)
 
         return carry
 

time: 45.7 us -> 46.3 us (1.013)
  Pallas kernels: 42.9 us -> 43.5 us
    pallas_call x1, Pallas kernels: 42.9 us -> 43.5 us  [local(): pl.pallas_call(functools.partial(kernel, n_segment, n_seq), out_shape=jax...]
where the time goes in v3:
time: 46.3 us; the launch traced here: 46 us
  Pallas kernels  43.5 us (94%)
  local copies, waits for them, and re-layouts  2.5 us (5%)
    pallas_call x1, Pallas kernels, local(): pl.pallas_call(functools.partial(kernel, n_segment, n_seq), out_shape=jax...  43.5 us
    unnamed x1, local copies, waits for them, and re-layouts  2.5 us

profile of v3, /device:TPU:17, one launch (start us, length us, event | category | flops | bytes accessed | tf_op | source)
XLA Modules:
  0.0 46.0 jit_solution(14278779535878618102)
XLA Ops:
  0.0 43.5 %shard_map.64 = bf16[1,4,2,8,16,640]{5,4,3,2,1,0:T(8,128)(2,1)} custom-call(bf16[1,2,8,16,640]{4,3,2,1,0:T(8,128)(2,1)} %held.1, bf16[3,2,8,16,640]{4,3,2,1,0:T(8,128)(2,1)} %arrivals.1, bf16[1,9,640,640]{3,2,1,0:T(8,128)(2,1)} %w_s.1, f32[5,1,640]{2,1,0:T(1,128)} %bitcast.2, bf16[1,3,640,640]{3,2,1,0:T(8,128)(2,1)} %w_t.1, f32[5,1,640]{2,1,0:T(1,128)} %bitcast.3), custom_call_target="tpu_custom_call" | custom-call | flops 10066329600 | bytes 9830400 | tf_op jit(solution)/shard_map/pallas_call | solution.py:236
  43.5 2.5 %copy.8 = bf16[1,4,2,8,16,640]{5,4,3,2,1,0:T(8,128)(2,1)} copy(bf16[1,4,2,8,16,640]{5,4,3,2,1,0:T(8,128)(2,1)} %shard_map.64) | data formatting | bytes 2621440

commit v4 on v3

--- a/solution.py
+++ b/solution.py
@@ -188,21 +188,12 @@
                 send_halo(0)
 
         spatial(t, False)
-        late = (segment == 0) & (t == ticks - 1)
-
-        @pl.when(jnp.logical_not(late))
-        def _():
-            send_halo(t)
-
+        send_halo(t)
         temporal(t - 1)
 
         @pl.when(has_down)
         def _():
             relay(t - 1).start()
-
-        @pl.when(late)
-        def _():
-            send_halo(t)
 
         return carry
 

time: 46.3 us -> 45.3 us (0.978)
  Pallas kernels: 43.5 us -> 42.2 us
    pallas_call x1, Pallas kernels: 43.5 us -> 42.2 us  [local(): pl.pallas_call(functools.partial(kernel, n_segment, n_seq), out_shape=jax...]
where the time goes in v4:
time: 45.3 us; the launch traced here: 44.7 us
  Pallas kernels  42.2 us (93%)
  local copies, waits for them, and re-layouts  2.5 us (6%)
    pallas_call x1, Pallas kernels, local(): pl.pallas_call(functools.partial(kernel, n_segment, n_seq), out_shape=jax...  42.2 us
    unnamed x1, local copies, waits for them, and re-layouts  2.5 us

profile of v4, /device:TPU:17, one launch (start us, length us, event | category | flops | bytes accessed | tf_op | source)
XLA Modules:
  0.0 44.7 jit_solution(7800870044128147720)
XLA Ops:
  0.0 42.2 %shard_map.64 = bf16[1,4,2,8,16,640]{5,4,3,2,1,0:T(8,128)(2,1)} custom-call(bf16[1,2,8,16,640]{4,3,2,1,0:T(8,128)(2,1)} %held.1, bf16[3,2,8,16,640]{4,3,2,1,0:T(8,128)(2,1)} %arrivals.1, bf16[1,9,640,640]{3,2,1,0:T(8,128)(2,1)} %w_s.1, f32[5,1,640]{2,1,0:T(1,128)} %bitcast.2, bf16[1,3,640,640]{3,2,1,0:T(8,128)(2,1)} %w_t.1, f32[5,1,640]{2,1,0:T(1,128)} %bitcast.3), custom_call_target="tpu_custom_call" | custom-call | flops 10066329600 | bytes 9830400 | tf_op jit(solution)/shard_map/pallas_call | solution.py:227
  42.2 2.5 %copy.8 = bf16[1,4,2,8,16,640]{5,4,3,2,1,0:T(8,128)(2,1)} copy(bf16[1,4,2,8,16,640]{5,4,3,2,1,0:T(8,128)(2,1)} %shard_map.64) | data formatting | bytes 2621440
